TPU v7x, 128 devices: a whole 4x4x4 slice. The times are simulated.
128 devices in a mesh: row: 8 (over z, core), col: 16 (over y, x).
Axes of the slice: x: 4, y: 4, z: 4, core: 2. Of those that a mesh axis runs over, the one named last changes fastest.
Arguments:
- integrals: bfloat16 [4096, 128, 2048], P('col', 'row'), may hold values from -6 to 6
- occupancy: int32 [32, 16], replicated, may hold values from 0 to 1
- coeffs: bfloat16 [2048, 256], replicated, may hold values from -0.125 to 0.125
- metric: bfloat16 [4096, 4096], P('col'), as said below
Outputs:
- fitted: bfloat16 [4096, 128, 256], P('col', 'row')
- pair_matrix: float32 [256, 256], replicated
Inputs may be any that keep to these rules, and one draw needn't show every extreme that they name: metric is symmetric.
All inputs are finite; a program needn't handle non-finite values.
Results may differ from a plain program's by a relative error of at most 0.0037.
The roundings to bfloat16 on the way count: a program that leaves them out, or rounds other values in their place, can miss the bound.
Values may be sent and summed in bfloat16 or wider, within the bound.
A program may use at most 192 MiB of HBM per device.

v0:
```python
import jax
import jax.numpy as jnp
from jax import lax
from jax.sharding import PartitionSpec as P

BLK = 128


def on_device(integrals, occupancy, coeffs, metric):
    rows = integrals.shape[0]
    mu_local = integrals.shape[1]
    basis = integrals.shape[2]
    orbitals = coeffs.shape[1]
    aux_blocks = rows // BLK
    nu_blocks = basis // BLK
    first = lax.axis_index("col") * aux_blocks
    local_mask = lax.dynamic_slice_in_dim(occupancy, first, aux_blocks, 0).astype(integrals.dtype)
    blocks = integrals.reshape(aux_blocks, BLK, mu_local, nu_blocks, BLK)
    masked = blocks * local_mask[:, None, None, :, None]
    half = jnp.dot(
        masked.reshape(rows * mu_local, basis), coeffs, preferred_element_type=jnp.float32
    ).astype(jnp.bfloat16)
    width = mu_local * orbitals
    half = half.reshape(rows, width)
    summed = jnp.dot(
        metric, lax.all_gather(half, "col", axis=0, tiled=True), preferred_element_type=jnp.float32
    )
    fitted = summed.astype(jnp.bfloat16)
    flat = fitted.reshape(rows * mu_local, orbitals)
    local_pairs = lax.dot_general(
        flat, flat, (((0,), (0,)), ((), ())), preferred_element_type=jnp.float32
    )
    total_pairs = lax.psum(local_pairs, ("row", "col"))
    count = rows * lax.axis_size("col") * mu_local * lax.axis_size("row")
    pair_matrix = total_pairs / jnp.float32(count)
    return (fitted.reshape(rows, mu_local, orbitals), pair_matrix)


def solution(mesh):
    placed = (P("col", "row", None), P(), P(), P("col", None))
    return jax.shard_map(
        on_device,
        mesh=mesh,
        in_specs=placed,
        out_specs=(P("col", "row", None), P()),
        check_vma=False,
    )
```

profile of v0, /device:TPU:1, one launch (start us, length us, event | category | flops | bytes accessed | tf_op | source)
XLA Modules:
  0.0 411.0 jit_solution(3826708779120821734)
XLA Ops:
  7.2 0.0 copy-start
  7.2 0.0 all-gather.2.cloned.1.call-start
  7.2 0.9 constant_dynamic-slice_fusion
  8.1 0.1 copy.14
  8.2 0.0 copy-start.2
  8.2 6.6 %mul.15 = bf16[2,128,16,16,128]{4,3,2,1,0:T(8,128)(2,1)} broadcast(bf16[2,16]{1,0:T(2,128)(2,1)S(1)} %convert_element_type.12), dimensions={0,3} | broadcast | bytes 16777280 | tf_op jit(solution)/shard_map/mul | solution.py:19
  14.8 0.0 copy-done.2
  14.8 15.5 %fusion.2 = bf16[4096,256]{1,0:T(8,128)(2,1)} fusion(bf16[2048,256]{1,0:T(8,128)(2,1)S(1)} %copy-done.2, bf16[4096,2048]{1,0:T(8,128)(2,1)} %bitcast.19, bf16[512,8,16,128]{3,2,1,0:T(8,128)(2,1)} %bitcast.16), kind=kOutput, calls=%fused_computation.3 | convolution fusion | flops 4304404480 | bytes 36700160 | tf_op jit(solution)/shard_map/dot_general | solution.py:20
  30.3 4.2 %reshape.21 = bf16[256,4096]{1,0:T(8,128)(2,1)} reshape(bf16[4096,256]{1,0:T(8,128)(2,1)} %fusion.2) | data formatting | bytes 4194304 | tf_op jit(solution)/shard_map/reshape | solution.py:24
  34.5 0.0 all-gather.2.cloned.1.call-update
  34.5 0.0 all-reduce.2.cloned.1.call-start
  34.6 200.3 %all-gather.2.cloned.1.call-done = bf16[4096,4096]{1,0:T(8,128)(2,1)} async-done(((bf16[256,4096]{1,0:T(8,128)(2,1)}), bf16[4096,4096]{1,0:T(8,128)(2,1)}) %all-gather.2.cloned.1.call-update) | async-done | bytes 33554448 | tf_op jit(solution)/shard_map/all_gather | solution.py:26
  234.8 0.0 copy-done
  234.8 17.2 %convolution_convert_fusion = bf16[4096,256]{1,0:T(8,128)(2,1)} fusion(bf16[4096,4096]{1,0:T(8,128)(2,1)} %all-gather.2.cloned.1.call-done, bf16[256,4096]{1,0:T(8,128)(2,1)S(1)} %copy-done), kind=kOutput, calls=%fused_computation.4 | convolution fusion | flops 8590983168 | bytes 37748736 | tf_op jit(solution)/shard_map/dot_general | solution.py:25
  252.1 2.9 copy.12
  255.0 2.3 reshape.23
  257.3 3.7 fusion.3
  261.0 0.0 all-reduce.2.cloned.1.call-update
  261.0 0.0 copy-start.1
  261.0 4.6 %copy.13 = bf16[256,16,256]{2,1,0:T(8,128)(2,1)} copy(bf16[256,16,256]{0,2,1:T(8,128)(2,1)} %bitcast.18) | data formatting | bytes 4194304
  265.7 136.8 %all-reduce.2.cloned.1.call-done = f32[256,256]{1,0:T(8,128)} async-done(((f32[256,256]{1,0:T(8,128)}), f32[256,256]{1,0:T(8,128)}) %all-reduce.2.cloned.1.call-update) | async-done | bytes 262160 | tf_op jit(solution)/shard_map/psum | solution.py:33
  402.5 1.7 broadcast_multiply_fusion
  404.1 0.0 copy-done.1
  (1 shorter events, 0.0 us)
Async XLA Ops:
  7.2 227.7 %copy-start = (bf16[256,4096]{1,0:T(8,128)(2,1)S(1)}, bf16[256,4096]{1,0:T(8,128)(2,1)}, u32[]{:S(2)}) copy-start(bf16[256,4096]{1,0:T(8,128)(2,1)} %param.7) | copy-start | bytes 6291460
  7.2 227.7 %all-gather.2.cloned.1.call-start = ((), (), s32[]{:S(2)}) async-start(), calls=%async_computation | async-start | bytes 35651584 | tf_op jit(solution)/shard_map/all_gather | solution.py:26
  8.2 6.6 %copy-start.2 = (bf16[2048,256]{1,0:T(8,128)(2,1)S(1)}, bf16[2048,256]{1,0:T(8,128)(2,1)}, u32[]{:S(2)}) copy-start(bf16[2048,256]{1,0:T(8,128)(2,1)} %param.6) | copy-start | bytes 3145732
  34.5 367.9 %all-reduce.2.cloned.1.call-start = ((), (), s32[]{:S(2)}) async-start(), calls=%async_computation.1 | async-start | bytes 524288 | tf_op jit(solution)/shard_map/psum | solution.py:33
  261.0 143.1 %copy-start.1 = (bf16[256,4096]{1,0:T(8,128)(2,1)S(1)}, bf16[256,4096]{1,0:T(8,128)(2,1)}, u32[]{:S(2)}) copy-start(bf16[256,4096]{1,0:T(8,128)(2,1)} %param.7) | copy-start | bytes 6291460
Sparse Core Ops, SparseCore 0:
  34.7 200.1 all-gather.1
  261.1 141.2 all-reduce.1
where the time goes:
time: 411 us
  waiting for transfers between devices  337 us (82%)
  matrix products  36.4 us (9%)
  local copies, waits for them, and re-layouts  21.7 us (5%)
  between operations  14.1 us (3%)
    all_gather x1, waiting for transfers between devices, on_device(): lax.all_gather(half, 'col', axis=0, tiled=True)  200 us
    psum x1, waiting for transfers between devices, on_device(): total_pairs = lax.psum(local_pairs, ('row', 'col'))  137 us
    dot_general x1, matrix products, on_device(): jnp.dot(metric, lax.all_gather(half, 'col', axis=0, tiled=True), preferre...  17.2 us
    dot_general x1, matrix products, on_device(): jnp.dot(masked.reshape(rows * mu_local, basis), coeffs, preferred_element...  15.5 us
  transfers between devices with their start and end apart: 2, of which 2 were waited for; matrix products, arithmetic and copies ran while one was open for 1% of the time, Pallas kernels for 0%

commit v1 on v0

v1 whole, which is shorter than its diff:
```python
import functools

import jax
import jax.numpy as jnp
from jax import lax
from jax.experimental import pallas as pl
from jax.experimental.pallas import tpu as pltpu
from jax.sharding import PartitionSpec as P

BLK = 128
NX = 4
NY = 4
QC = 32
UNIT = 2
AHEAD = 2
LAG = 1
NBUF = 4
OPP, RIGHT, LEFT, OWN = range(4)
MESH = pl.DeviceIdType.MESH
F32 = jnp.float32
BF16 = jnp.bfloat16


def kernel(
    dims, integrals, occupancy, coeffs, metric, fitted, pair,
    ibuf, cbuf, cmask, stage_a, stage_b, mb, mbt, hbuf, opp_out, side_out, opp_in, side_in,
    rows_f32, out_bf16, pbuf, pair_acc, red0, mine, red1, red2, red3, red4,
    in_sem, c_sem, m_loc, m_send, m_recv, m2_send, m2_recv, m3_send, m3_recv,
    ag_send, ag_recv, fw_send, fw_recv, op_send, op_recv, sd_send, sd_recv,
    r0_send, r0_recv, r1_send, r1_recv, r2_send, r2_recv, r3_send, r3_recv,
    r4_send, r4_recv, out_sem,
):
    ncol, nrow, rows, nmu, basis, no, scale = dims
    half = rows // 2
    kq = NX * rows
    per_set = nmu // 2
    nset = per_set // UNIT
    nz = nrow // 2
    row = lax.axis_index("row")
    sib = row + 1 - 2 * lax.rem(row, 2)
    col = lax.axis_index("col")
    x = lax.rem(col, NX)
    y = lax.div(col, NX)
    nab = rows // BLK
    nch = rows // QC

    def col_x(d):
        return y * NX + lax.rem(x + d, NX)

    def col_y(d):
        return lax.rem(y + d, NY) * NX + x

    ag_to = ((col_x(1), col_x(NX - 1)), (col_y(1), col_y(NY - 1)))
    rs_to = (ag_to[1], ag_to[0])
    at_x = tuple(lax.rem(x + d, NX) for d in (0, NX - 1, 1, 2))
    held = (at_x, (OWN, LEFT, RIGHT, OPP))

    def in_copy(ch):
        q = pl.ds(ch * QC, QC)
        slot = lax.rem(ch, NBUF)
        return pltpu.make_async_copy(integrals.at[q], ibuf.at[slot], in_sem.at[slot])

    c_copy = pltpu.make_async_copy(coeffs, cbuf, c_sem)
    c_copy.start()

    @pl.loop(0, NBUF)
    def _(ch):
        in_copy(ch).start()

    def m_own():
        src = metric.at[:, pl.ds(pl.multiple_of(y * kq, 128), kq)]
        return pltpu.make_async_copy(src, mb.at[OWN], m_loc)

    m_own().start()

    barrier = pltpu.get_barrier_semaphore()

    @pl.loop(1, ncol)
    def _(d):
        pl.semaphore_signal(
            barrier, inc=1, device_id=(row, lax.rem(col + d, ncol)), device_id_type=MESH
        )

    @pl.loop(1, nrow)
    def _(d):
        pl.semaphore_signal(
            barrier, inc=1, device_id=(lax.rem(row + d, nrow), col), device_id_type=MESH
        )

    slot_of = {1: RIGHT, 2: OPP, 3: LEFT}
    share = rows // nrow

    def rows_of(r):
        return pl.ds(pl.multiple_of(r * share, 16), share)

    def m_copy(d):
        yd = lax.rem(y + d, NY)
        return pltpu.make_async_remote_copy(
            src_ref=metric.at[rows_of(row), pl.ds(pl.multiple_of(yd * kq, 128), kq)],
            dst_ref=mb.at[slot_of[NY - d], rows_of(row)],
            send_sem=m_send.at[d - 1],
            recv_sem=m_recv.at[NY - d - 1],
            device_id=(row, col_y(d)),
            device_id_type=MESH,
        )

    def m_landed(s):
        return pltpu.make_async_remote_copy(
            src_ref=metric.at[rows_of(row), pl.ds(0, kq)],
            dst_ref=mb.at[slot_of[s], rows_of(row)],
            send_sem=m_send.at[s - 1],
            recv_sem=m_recv.at[s - 1],
            device_id=(row, col_y(s)),
            device_id_type=MESH,
        )

    def along_z(d):
        return lax.rem(row + 2 * d, nrow)

    def m_share(s, d):
        blk = mb.at[slot_of[s], rows_of(row)]
        return pltpu.make_async_remote_copy(
            src_ref=blk,
            dst_ref=blk,
            send_sem=m2_send.at[s - 1, d - 1],
            recv_sem=m2_recv.at[s - 1, nz - d - 1],
            device_id=(along_z(d), col),
            device_id_type=MESH,
        )

    def m_shared(s, d):
        blk = mb.at[slot_of[s], rows_of(along_z(d))]
        return pltpu.make_async_remote_copy(
            src_ref=blk,
            dst_ref=blk,
            send_sem=m2_send.at[s - 1, d - 1],
            recv_sem=m2_recv.at[s - 1, d - 1],
            device_id=(along_z(d), col),
            device_id_type=MESH,
        )

    def m_pass(s, d, mine=True):
        src = along_z(d) if mine else lax.rem(sib + 2 * d, nrow)
        blk = mb.at[slot_of[s], rows_of(src)]
        return pltpu.make_async_remote_copy(
            src_ref=blk,
            dst_ref=blk,
            send_sem=m3_send.at[s - 1, d],
            recv_sem=m3_recv.at[s - 1, d],
            device_id=(sib, col),
            device_id_type=MESH,
        )

    c_copy.wait()
    for ab in range(nab):

        @pl.loop(0, basis // BLK, unroll=4)
        def _(nb):
            on = jnp.full((BLK, no), occupancy[nb, col * nab + ab], jnp.int32) > 0
            at = pl.ds(pl.multiple_of(nb * BLK, BLK), BLK)
            kept = jnp.where(on, cbuf[at, :].astype(F32), 0.0)
            cmask[ab, at, :] = kept.astype(BF16)

    pl.semaphore_wait(barrier, ncol + nrow - 2)

    for d in (2, 1, 3):
        m_copy(d).start()

    def transform(ch, ab, to):
        rowsin = ibuf[lax.rem(ch, NBUF)].reshape(QC * nmu, basis)
        res = jnp.dot(rowsin, cmask[ab], preferred_element_type=F32)
        for h in range(no // 128):
            to[h] = res[:, h * 128 : (h + 1) * 128]

    def relayout(ch, frm):
        q0 = pl.multiple_of(ch * QC, QC)
        for mu in range(nmu):
            own = held[mu // per_set][0]
            for h in range(no // 128):
                got = frm[h, pl.ds(mu, QC, stride=nmu), :]
                hbuf[mu, own, pl.ds(q0, QC), h * 128 : (h + 1) * 128] = got.astype(BF16)

    def mus(st, k):
        return pl.ds(st * per_set + k * UNIT, UNIT)

    def ag_copy(st, side, k, hf, blk=None, to=None):
        part_rows = pl.ds(hf * half, half)
        src = held[st][0] if blk is None else blk
        dst = (at_x[0], (LEFT, RIGHT)[side])[st] if to is None else to
        return pltpu.make_async_remote_copy(
            src_ref=hbuf.at[mus(st, k), src, part_rows],
            dst_ref=hbuf.at[mus(st, k), dst, part_rows],
            send_sem=ag_send.at[st, side, k, hf],
            recv_sem=ag_recv.at[st, side, k, hf],
            device_id=(row, ag_to[st][side]),
            device_id_type=MESH,
        )

    def ag_wait(st, side, k, hf):
        blk = held[st][1 + side]
        ag_copy(st, side, k, hf, blk, blk).wait_recv()

    def fw_copy(st, side, k, blk=None, to=None):
        part_rows = pl.ds(side * half, half)
        src = held[st][1 + side] if blk is None else blk
        dst = (at_x[1 + side], OPP)[st] if to is None else to
        return pltpu.make_async_remote_copy(
            src_ref=hbuf.at[mus(st, k), src, part_rows],
            dst_ref=hbuf.at[mus(st, k), dst, part_rows],
            send_sem=fw_send.at[st, side, k],
            recv_sem=fw_recv.at[st, side, k],
            device_id=(row, ag_to[st][side]),
            device_id_type=MESH,
        )

    def fw_wait(st, side, k):
        blk = held[st][3]
        fw_copy(st, side, k, blk, blk).wait_recv()

    def op_copy(st, side, k):
        part_rows = pl.ds(side * half, half)
        return pltpu.make_async_remote_copy(
            src_ref=opp_out.at[mus(st, k), part_rows],
            dst_ref=opp_in.at[mus(st, k), part_rows],
            send_sem=op_send.at[st, side, k],
            recv_sem=op_recv.at[st, side, k],
            device_id=(row, rs_to[st][side]),
            device_id_type=MESH,
        )

    def sd_copy(st, side, mu):
        return pltpu.make_async_remote_copy(
            src_ref=side_out.at[side, mu],
            dst_ref=side_in.at[side, mu],
            send_sem=sd_send.at[side, mu],
            recv_sem=sd_recv.at[side, mu],
            device_id=(row, rs_to[st][side]),
            device_id_type=MESH,
        )

    def ag_start(st, k):
        for step in range(2):
            ag_copy(st, 0, k, step).start()
            ag_copy(st, 1, k, 1 - step).start()

    def forward(st, k):
        for side in range(2):
            ag_wait(st, side, k, side)
            fw_copy(st, side, k).start()

    def product(st, k):
        block = (mb, mbt)[st]
        for side in range(2):
            ag_wait(st, side, k, 1 - side)
            fw_wait(st, side, k)

        @pl.loop(0, UNIT)
        def _(m):
            mu = st * per_set + k * UNIT + m
            full = hbuf[mu].reshape(kq, no)
            got = jnp.dot(block[...].reshape(NY * rows, kq), full, preferred_element_type=F32)
            opp_out[mu] = got[:rows].astype(BF16)
            for side in range(2):
                at = (1 + side) * rows
                first = got[at : at + half]
                second = got[at + half : at + rows]
                plain = pl.ds((1 - side) * half, half)
                side_out[side, mu, plain] = (second, first)[side].astype(BF16)
                pbuf[st, lax.rem(k, 3), m, pl.ds(side * half, half)] = (first, second)[side]
            pbuf[st, lax.rem(k, 3), m, pl.ds(rows, rows)] = got[3 * rows :]

        op_copy(st, 0, k).start()
        op_copy(st, 1, k).start()

    def sides(k):
        for m in range(UNIT):
            for st in range(2):
                mu = st * per_set + k * UNIT + m
                for side in range(2):
                    if m == 0:
                        op_copy(st, side, k).wait_recv()
                    at = pl.ds(side * half, half)
                    side_out[side, mu, at] = (
                        pbuf[st, lax.rem(k, 3), m, at] + opp_in[mu, at].astype(F32)
                    ).astype(BF16)
                    sd_copy(st, side, mu).start()

    pair_acc[...] = jnp.zeros_like(pair_acc)

    def finish(k):
        @pl.loop(0, UNIT)
        def _(m):
            pairs = []
            for st in range(2):
                for side in range(2):
                    sd_copy(st, side, st * per_set + k * UNIT + m).wait_recv()
            for st in range(2):
                mu = st * per_set + k * UNIT + m
                own = pbuf[st, lax.rem(k, 3), m, pl.ds(rows, rows)]
                total = own + side_in[0, mu].astype(F32) + side_in[1, mu].astype(F32)
                done = total.astype(BF16)
                back = done.astype(F32)
                for h in range(no // 128):
                    at = pl.ds(mu, rows, stride=nmu)
                    rows_f32[h, at, :] = back[:, h * 128 : (h + 1) * 128]
                pairs.append(done)
            both = jnp.concatenate(pairs, axis=0)
            pair_acc[...] += lax.dot_general(
                both, both, (((0,), (0,)), ((), ())), preferred_element_type=F32
            )

    quarter = rows // 4

    def send_quarter(qt):
        part_rows = pl.ds(pl.multiple_of(qt * quarter, quarter), quarter)
        for k in range(AHEAD):
            for st in range(2):
                for side in range(2):
                    pltpu.make_async_remote_copy(
                        src_ref=hbuf.at[mus(st, k), held[st][0], part_rows],
                        dst_ref=hbuf.at[
                            mus(st, k), (at_x[0], (LEFT, RIGHT)[side])[st], part_rows
                        ],
                        send_sem=ag_send.at[st, side, k, lax.div(qt, 2)],
                        recv_sem=ag_recv.at[st, side, k, lax.div(qt, 2)],
                        device_id=(row, ag_to[st][side]),
                        device_id_type=MESH,
                    ).start()

    stage_b[...] = jnp.zeros_like(stage_b)

    @pl.loop(0, nch // 2)
    def _(j):
        ch = 2 * j
        ab = lax.div(ch * QC, BLK)
        in_copy(ch).wait()
        in_copy(ch + 1).wait()
        transform(ch, ab, stage_a)
        relayout(lax.max(ch - 1, 0), stage_b)

        @pl.when(j >= 1)
        def _():
            send_quarter(j - 1)

        @pl.when(j == 1)
        def _():
            for s in (2, 1, 3):
                m_landed(s).wait_recv()
                for d in (2, 1, 3):
                    m_share(s, d).start()
                m_pass(s, 0).start()

        transform(ch + 1, ab, stage_b)
        relayout(ch, stage_a)

        @pl.when(ch + NBUF < nch)
        def _():
            in_copy(ch + NBUF).start()
            in_copy(ch + NBUF + 1).start()

    relayout(nch - 1, stage_b)
    send_quarter(nch // 2 - 1)

    def metric_sent():
        for s in range(1, NY):
            m_copy(s).wait_send()
            for d in range(nz):
                m_pass(s, d).wait_send()
            for d in range(1, nz):
                m_share(s, d).wait_send()

    def sent_early(k):
        for st in range(2):
            for side in range(2):
                for hf in range(2):
                    ag_copy(st, side, k, hf).wait_send()
                fw_copy(st, side, k).wait_send()
                op_copy(st, side, k).wait_send()

    def sent_late(k):
        for st in range(2):
            for side in range(2):
                for m in range(UNIT):
                    sd_copy(st, side, st * per_set + k * UNIT + m).wait_send()

    def metric_ready():
        m_own().wait()
        for d in range(nz):
            for s in (2, 1, 3):
                m_pass(s, d, False).wait_recv()

    def transpose_metric():
        offs = {OPP: 2, RIGHT: 1, LEFT: NX - 1, OWN: 0}
        for to, d in offs.items():
            at = pl.ds(pl.multiple_of(lax.rem(x + d, NX) * rows, 128), rows)

            @pl.loop(0, NY)
            def _(s):
                mbt[to, :, pl.ds(pl.multiple_of(s * rows, 128), rows)] = mb[s, :, at].T

    @pl.loop(0, nset + LAG + 2)
    def _(k):
        @pl.when(k + AHEAD < nset)
        def _():
            ag_start(0, k + AHEAD)
            ag_start(1, k + AHEAD)

        @pl.when(k < nset)
        def _():
            forward(0, k)
            forward(1, k)

        @pl.when(k == 0)
        def _():
            for s in (2, 1, 3):
                for d in (1, 3, 2):
                    m_shared(s, d).wait_recv()
                    m_pass(s, d).start()

        @pl.when((k >= LAG) & (k < nset + LAG))
        def _():
            @pl.when(k == LAG)
            def _():
                metric_ready()

            product(0, k - LAG)

            @pl.when(k == LAG)
            def _():
                transpose_metric()

            product(1, k - LAG)

        @pl.when((k >= LAG + 1) & (k < nset + LAG + 1))
        def _():
            sides(k - LAG - 1)
            sent_early(k - LAG - 1)

        @pl.when(k == LAG + 1)
        def _():
            metric_sent()

        @pl.when(k >= LAG + 2)
        def _():
            finish(k - LAG - 2)

        @pl.when((k >= LAG + 2) & (k < nset + LAG + 1))
        def _():
            sent_late(k - LAG - 2)

    chunk = no // 2 // ncol
    core = lax.rem(row, 2)
    mid = no // 2
    mine_at = pl.ds(pl.multiple_of(core * mid, 8), mid)
    theirs_at = pl.ds(pl.multiple_of((1 - core) * mid, 8), mid)

    r0_copy = pltpu.make_async_remote_copy(
        src_ref=pair_acc.at[theirs_at],
        dst_ref=red0,
        send_sem=r0_send,
        recv_sem=r0_recv,
        device_id=(sib, col),
        device_id_type=MESH,
    )
    r0_copy.start()

    def r1_copy(d):
        to = lax.rem(col + d, ncol)
        return pltpu.make_async_remote_copy(
            src_ref=mine.at[to],
            dst_ref=red1.at[col],
            send_sem=r1_send.at[d],
            recv_sem=r1_recv.at[col],
            device_id=(row, to),
            device_id_type=MESH,
        )

    def r1_landed(src):
        return pltpu.make_async_remote_copy(
            src_ref=mine.at[src],
            dst_ref=red1.at[src],
            send_sem=r1_send.at[0],
            recv_sem=r1_recv.at[src],
            device_id=(row, src),
            device_id_type=MESH,
        )

    def r2_copy(d):
        z = lax.div(row, 2)
        return pltpu.make_async_remote_copy(
            src_ref=red2.at[z],
            dst_ref=red2.at[z],
            send_sem=r2_send.at[d],
            recv_sem=r2_recv.at[z],
            device_id=(along_z(d), col),
            device_id_type=MESH,
        )

    def r2_landed(d):
        z = lax.div(along_z(d), 2)
        return pltpu.make_async_remote_copy(
            src_ref=red2.at[z],
            dst_ref=red2.at[z],
            send_sem=r2_send.at[d],
            recv_sem=r2_recv.at[z],
            device_id=(along_z(d), col),
            device_id_type=MESH,
        )

    def r3_copy(d):
        to = lax.rem(col + d, ncol)
        return pltpu.make_async_remote_copy(
            src_ref=red3.at[col],
            dst_ref=red3.at[col],
            send_sem=r3_send.at[d],
            recv_sem=r3_recv.at[col],
            device_id=(row, to),
            device_id_type=MESH,
        )

    def r3_landed(src):
        return pltpu.make_async_remote_copy(
            src_ref=red3.at[src],
            dst_ref=red3.at[src],
            send_sem=r3_send.at[0],
            recv_sem=r3_recv.at[src],
            device_id=(row, src),
            device_id_type=MESH,
        )

    def lay_out(begin, end):
        @pl.loop(begin, end)
        def _(ch):
            at = pl.ds(pl.multiple_of(ch * QC * nmu, QC), QC * nmu)
            for h in range(no // 128):
                out_bf16[pl.ds(ch * QC, QC), :, h * 128 : (h + 1) * 128] = (
                    rows_f32[h, at, :].astype(BF16).reshape(QC, nmu, 128)
                )

    lay_out(0, nch // 4)
    r0_copy.wait_recv()
    mine[...] = (pair_acc[mine_at] + red0[...]).reshape(ncol, chunk, no)

    @pl.loop(1, ncol, unroll=5)
    def _(d):
        r1_copy(d).start()

    red1[col] = mine[col]

    lay_out(nch // 4, nch)
    sent_late(nset - 1)

    out_copy = pltpu.make_async_copy(out_bf16, fitted, out_sem)
    out_copy.start()

    @pl.loop(1, ncol)
    def _(d):
        r1_landed(lax.rem(col + d, ncol)).wait_recv()

    total = red1[0]
    for c in range(1, ncol):
        total = total + red1[c]
    red2[lax.div(row, 2)] = total
    for d in (2, 1, 3):
        r2_copy(d).start()
    for d in (1, 3, 2):
        r2_landed(d).wait_recv()

    total = red2[0]
    for z in range(1, nz):
        total = total + red2[z]
    red3[col] = total * F32(scale)

    @pl.loop(1, ncol, unroll=5)
    def _(d):
        r3_copy(d).start()

    @pl.loop(1, ncol, unroll=5)
    def _(d):
        r3_landed(lax.rem(col + d, ncol)).wait_recv()

    r4_copy = pltpu.make_async_remote_copy(
        src_ref=red3,
        dst_ref=red4,
        send_sem=r4_send,
        recv_sem=r4_recv,
        device_id=(sib, col),
        device_id_type=MESH,
    )
    r4_copy.start()
    pair[mine_at] = red3[...].reshape(mid, no)

    r0_copy.wait_send()

    @pl.loop(1, ncol)
    def _(d):
        r1_copy(d).wait_send()
        r3_copy(d).wait_send()

    for d in range(1, nz):
        r2_copy(d).wait_send()

    r4_copy.wait_recv()
    pair[theirs_at] = red4[...].reshape(mid, no)
    r4_copy.wait_send()
    out_copy.wait()


def on_device(ncol, nrow, integrals, occupancy, coeffs, metric):
    rows, nmu, basis = integrals.shape
    no = coeffs.shape[1]
    kq = NX * rows
    chunk = no // 2 // ncol
    scale = 1.0 / (rows * ncol * nmu * nrow)
    dims = (ncol, nrow, rows, nmu, basis, no, scale)
    lanes = no // 128
    dma = pltpu.SemaphoreType.DMA
    scratch = [
        pltpu.VMEM((NBUF, QC, nmu, basis), BF16),
        pltpu.VMEM((basis, no), BF16),
        pltpu.VMEM((rows // BLK, basis, no), BF16),
        pltpu.VMEM((lanes, QC * nmu, 128), F32),
        pltpu.VMEM((lanes, QC * nmu, 128), F32),
        pltpu.VMEM((NY, rows, kq), BF16),
        pltpu.VMEM((NX, rows, kq), BF16),
        pltpu.VMEM((nmu, NX, rows, no), BF16),
        pltpu.VMEM((nmu, rows, no), BF16),
        pltpu.VMEM((2, nmu, rows, no), BF16),
        pltpu.VMEM((nmu, rows, no), BF16),
        pltpu.VMEM((2, nmu, rows, no), BF16),
        pltpu.VMEM((lanes, rows * nmu, 128), F32),
        pltpu.VMEM((rows, nmu, no), BF16),
        pltpu.VMEM((2, 3, UNIT, 2 * rows, no), F32),
        pltpu.VMEM((no, no), F32),
        pltpu.VMEM((no // 2, no), F32),
        pltpu.VMEM((ncol, chunk, no), F32),
        pltpu.VMEM((ncol, chunk, no), F32),
        pltpu.VMEM((nrow // 2, chunk, no), F32),
        pltpu.VMEM((ncol, chunk, no), F32),
        pltpu.VMEM((ncol, chunk, no), F32),
        dma((NBUF,)),
        dma,
        dma,
        dma((NY - 1,)),
        dma((NY - 1,)),
        dma((NY - 1, nrow // 2 - 1)),
        dma((NY - 1, nrow // 2 - 1)),
        dma((NY - 1, nrow // 2)),
        dma((NY - 1, nrow // 2)),
        dma((2, 2, nmu // 2 // UNIT, 2)),
        dma((2, 2, nmu // 2 // UNIT, 2)),
        dma((2, 2, nmu // 2 // UNIT)),
        dma((2, 2, nmu // 2 // UNIT)),
        dma((2, 2, nmu // 2 // UNIT)),
        dma((2, 2, nmu // 2 // UNIT)),
        dma((2, nmu)),
        dma((2, nmu)),
        dma,
        dma,
        dma((ncol,)),
        dma((ncol,)),
        dma((nrow // 2,)),
        dma((nrow // 2,)),
        dma((ncol,)),
        dma((ncol,)),
        dma,
        dma,
        dma,
    ]
    anywhere = pl.BlockSpec(memory_space=pl.ANY)
    flops = 2 * rows * nmu * no * (basis + ncol * rows + no)
    return pl.pallas_call(
        functools.partial(kernel, dims),
        out_shape=(
            pltpu.VMEM((rows, nmu, no), BF16),
            pltpu.VMEM((no, no), F32),
        ),
        in_specs=[
            anywhere,
            pl.BlockSpec(memory_space=pltpu.SMEM),
            anywhere,
            anywhere,
        ],
        out_specs=(anywhere, pl.BlockSpec(memory_space=pltpu.VMEM)),
        scratch_shapes=scratch,
        compiler_params=pltpu.CompilerParams(
            collective_id=0, has_side_effects=True, vmem_limit_bytes=58 * 1024 * 1024
        ),
        cost_estimate=pl.CostEstimate(
            flops=flops, bytes_accessed=2 * rows * nmu * (basis + no), transcendentals=0
        ),
    )(integrals, occupancy.T, coeffs, metric)


def solution(mesh):
    placed = (P("col", "row", None), P(), P(), P("col", None))
    return jax.shard_map(
        functools.partial(on_device, mesh.shape["col"], mesh.shape["row"]),
        mesh=mesh,
        in_specs=placed,
        out_specs=(P("col", "row", None), P()),
        check_vma=False,
    )
```

time: 411 us -> 105 us (0.26)
  waiting for transfers between devices: 337 us -> 0 us
  Pallas kernels: 0 us -> 103 us
  matrix products: 36.4 us -> 0 us
  local copies, waits for them, and re-layouts: 21.7 us -> 2.02 us
  between operations: 14.1 us -> 0.64 us
    all_gather x1 -> x0, waiting for transfers between devices: 200 us -> none  [on_device(): lax.all_gather(half, 'col', axis=0, tiled=True)]
    psum x1 -> x0, waiting for transfers between devices: 137 us -> none  [on_device(): total_pairs = lax.psum(local_pairs, ('row', 'col'))]
    pallas_call x0 -> x1, Pallas kernels: none -> 103 us  [on_device(): pl.pallas_call(functools.partial(kernel, dims), out_shape=(pltpu.VMEM((ro...]
    dot_general x3 -> x0, matrix products: 36.4 us -> none  [the longest x1 17.2 us: on_device(): jnp.dot(metric, lax.all_gather(half, 'col', axis=0, tiled=True), preferre...]
    mul x1 -> x0, local copies, waits for them, and re-layouts: 6.6 us -> none  [on_device(): masked = blocks * local_mask[:, None, None, :, None]]
    reshape x2 -> x0, local copies, waits for them, and re-layouts: 6.54 us -> none  [the longest x1 4.2 us: on_device(): half = half.reshape(rows, width)]
  transfers between devices with their start and end apart: 2 -> 0, of which waited for: 2 -> 0; matrix products, arithmetic and copies ran while one was open for 1% -> 0% of each run, Pallas kernels for 0% -> 0%
where the time goes in v1:
time: 105 us
  Pallas kernels  103 us (98%)
  local copies, waits for them, and re-layouts  2.02 us (2%)
    pallas_call x1, Pallas kernels, on_device(): pl.pallas_call(functools.partial(kernel, dims), out_shape=(pltpu.VMEM((ro...  103 us

profile of v1, /device:TPU:1, one launch (start us, length us, event | category | flops | bytes accessed | tf_op | source)
XLA Modules:
  0.0 105.3 jit_solution(14758128940296341187)
XLA Ops:
  0.6 102.6 %shard_map.59 = (bf16[256,16,256]{2,1,0:T(8,128)(2,1)S(1)}, f32[256,256]{1,0:T(8,128)S(1)}) custom-call(bf16[256,16,2048]{2,1,0:T(8,128)(2,1)} %integrals.1, s32[16,32]{1,0:T(8,128)} %bitcast.1, bf16[2048,256]{1,0:T(8,128)(2,1)} %coeffs.1, bf16[256,4096]{1,0:T(8,128)(2,1)} %metric.1), custom_call_target="tpu_custom_call" | custom-call | flops 13421772800 | bytes 18874368 | tf_op jit(solution)/shard_map/pallas_call | solution.py:672
  103.3 1.3 %copy.8 = bf16[256,16,256]{2,1,0:T(8,128)(2,1)} copy(bf16[256,16,256]{2,1,0:T(8,128)(2,1)S(1)} %get-tuple-element.2) | data formatting | bytes 4194304
  104.6 0.7 copy.9

commit v2 on v1

--- a/solution.py
+++ b/solution.py
@@ -152,14 +152,15 @@
         )
 
     c_copy.wait()
-    for ab in range(nab):
-
+    def make_mask(ab):
         @pl.loop(0, basis // BLK, unroll=4)
         def _(nb):
             on = jnp.full((BLK, no), occupancy[nb, col * nab + ab], jnp.int32) > 0
             at = pl.ds(pl.multiple_of(nb * BLK, BLK), BLK)
             kept = jnp.where(on, cbuf[at, :].astype(F32), 0.0)
             cmask[ab, at, :] = kept.astype(BF16)
+
+    make_mask(0)
 
     pl.semaphore_wait(barrier, ncol + nrow - 2)
 
@@ -333,6 +334,13 @@
     def _(j):
         ch = 2 * j
         ab = lax.div(ch * QC, BLK)
+
+        for later in range(1, nab):
+
+            @pl.when(ch == later * (nch // nab))
+            def _():
+                make_mask(later)
+
         in_copy(ch).wait()
         in_copy(ch + 1).wait()
         transform(ch, ab, stage_a)
@@ -417,6 +425,10 @@
                     m_shared(s, d).wait_recv()
                     m_pass(s, d).start()
 
+        @pl.when(k == nset + LAG - 1)
+        def _():
+            sides(k - LAG - 1)
+
         @pl.when((k >= LAG) & (k < nset + LAG))
         def _():
             @pl.when(k == LAG)
@@ -431,9 +443,12 @@
 
             product(1, k - LAG)
 
+        @pl.when((k >= LAG + 1) & (k < nset + LAG + 1) & (k != nset + LAG - 1))
+        def _():
+            sides(k - LAG - 1)
+
         @pl.when((k >= LAG + 1) & (k < nset + LAG + 1))
         def _():
-            sides(k - LAG - 1)
             sent_early(k - LAG - 1)
 
         @pl.when(k == LAG + 1)

time: 105 us -> 107 us (1.019)
    pallas_call x1, Pallas kernels: 103 us -> 104 us  [on_device(): pl.pallas_call(functools.partial(kernel, dims), out_shape=(pltpu.VMEM((ro...]
where the time goes in v2:
time: 107 us
  Pallas kernels  104 us (97%)
  local copies, waits for them, and re-layouts  2.02 us (2%)
    pallas_call x1, Pallas kernels, on_device(): pl.pallas_call(functools.partial(kernel, dims), out_shape=(pltpu.VMEM((ro...  104 us

profile of v2, /device:TPU:1, one launch (start us, length us, event | category | flops | bytes accessed | tf_op | source)
XLA Modules:
  0.0 107.1 jit_solution(4854889587735733593)
XLA Ops:
  0.6 104.4 %shard_map.59 = (bf16[256,16,256]{2,1,0:T(8,128)(2,1)S(1)}, f32[256,256]{1,0:T(8,128)S(1)}) custom-call(bf16[256,16,2048]{2,1,0:T(8,128)(2,1)} %integrals.1, s32[16,32]{1,0:T(8,128)} %bitcast.1, bf16[2048,256]{1,0:T(8,128)(2,1)} %coeffs.1, bf16[256,4096]{1,0:T(8,128)(2,1)} %metric.1), custom_call_target="tpu_custom_call" | custom-call | flops 13421772800 | bytes 18874368 | tf_op jit(solution)/shard_map/pallas_call | solution.py:687
  105.0 1.3 %copy.8 = bf16[256,16,256]{2,1,0:T(8,128)(2,1)} copy(bf16[256,16,256]{2,1,0:T(8,128)(2,1)S(1)} %get-tuple-element.2) | data formatting | bytes 4194304
  106.4 0.7 copy.9

commit v3 on v1

--- a/solution.py
+++ b/solution.py
@@ -384,34 +384,35 @@
                     sd_copy(st, side, st * per_set + k * UNIT + m).wait_send()
 
     def metric_ready():
-        m_own().wait()
         for d in range(nz):
             for s in (2, 1, 3):
                 m_pass(s, d, False).wait_recv()
 
-    def transpose_metric():
+    def transpose_metric(begin, end):
         offs = {OPP: 2, RIGHT: 1, LEFT: NX - 1, OWN: 0}
         for to, d in offs.items():
             at = pl.ds(pl.multiple_of(lax.rem(x + d, NX) * rows, 128), rows)
 
-            @pl.loop(0, NY)
+            @pl.loop(begin, end)
             def _(s):
                 mbt[to, :, pl.ds(pl.multiple_of(s * rows, 128), rows)] = mb[s, :, at].T
 
     @pl.loop(0, nset + LAG + 2)
     def _(k):
+        @pl.when(k < nset)
+        def _():
+            forward(0, k)
+            forward(1, k)
+
         @pl.when(k + AHEAD < nset)
         def _():
             ag_start(0, k + AHEAD)
             ag_start(1, k + AHEAD)
 
-        @pl.when(k < nset)
-        def _():
-            forward(0, k)
-            forward(1, k)
-
         @pl.when(k == 0)
         def _():
+            m_own().wait()
+            transpose_metric(OWN, OWN + 1)
             for s in (2, 1, 3):
                 for d in (1, 3, 2):
                     m_shared(s, d).wait_recv()
@@ -427,7 +428,7 @@
 
             @pl.when(k == LAG)
             def _():
-                transpose_metric()
+                transpose_metric(OPP, OWN)
 
             product(1, k - LAG)
 

time: 105 us -> 105 us (level)
  no operation moved by 1% of the time
where the time goes in v3:
time: 105 us
  Pallas kernels  103 us (98%)
  local copies, waits for them, and re-layouts  2.02 us (2%)
    pallas_call x1, Pallas kernels, on_device(): pl.pallas_call(functools.partial(kernel, dims), out_shape=(pltpu.VMEM((ro...  103 us

profile of v3, /device:TPU:1, one launch (start us, length us, event | category | flops | bytes accessed | tf_op | source)
XLA Modules:
  0.0 105.3 jit_solution(15491543532634127881)
XLA Ops:
  0.6 102.7 %shard_map.59 = (bf16[256,16,256]{2,1,0:T(8,128)(2,1)S(1)}, f32[256,256]{1,0:T(8,128)S(1)}) custom-call(bf16[256,16,2048]{2,1,0:T(8,128)(2,1)} %integrals.1, s32[16,32]{1,0:T(8,128)} %bitcast.1, bf16[2048,256]{1,0:T(8,128)(2,1)} %coeffs.1, bf16[256,4096]{1,0:T(8,128)(2,1)} %metric.1), custom_call_target="tpu_custom_call" | custom-call | flops 13421772800 | bytes 18874368 | tf_op jit(solution)/shard_map/pallas_call | solution.py:673
  103.3 1.3 %copy.8 = bf16[256,16,256]{2,1,0:T(8,128)(2,1)} copy(bf16[256,16,256]{2,1,0:T(8,128)(2,1)S(1)} %get-tuple-element.2) | data formatting | bytes 4194304
  104.6 0.7 copy.9

commit v4 on v1

--- a/solution.py
+++ b/solution.py
@@ -254,20 +254,21 @@
             ag_wait(st, side, k, 1 - side)
             fw_wait(st, side, k)
 
-        @pl.loop(0, UNIT)
-        def _(m):
-            mu = st * per_set + k * UNIT + m
-            full = hbuf[mu].reshape(kq, no)
-            got = jnp.dot(block[...].reshape(NY * rows, kq), full, preferred_element_type=F32)
-            opp_out[mu] = got[:rows].astype(BF16)
+        base = st * per_set + k * UNIT
+        full = jnp.concatenate([hbuf[base + m].reshape(kq, no) for m in range(UNIT)], axis=1)
+        got = jnp.dot(block[...].reshape(NY * rows, kq), full, preferred_element_type=F32)
+        for m in range(UNIT):
+            mu = base + m
+            lanes = slice(m * no, (m + 1) * no)
+            opp_out[mu] = got[:rows, lanes].astype(BF16)
             for side in range(2):
                 at = (1 + side) * rows
-                first = got[at : at + half]
-                second = got[at + half : at + rows]
+                first = got[at : at + half, lanes]
+                second = got[at + half : at + rows, lanes]
                 plain = pl.ds((1 - side) * half, half)
                 side_out[side, mu, plain] = (second, first)[side].astype(BF16)
                 pbuf[st, lax.rem(k, 3), m, pl.ds(side * half, half)] = (first, second)[side]
-            pbuf[st, lax.rem(k, 3), m, pl.ds(rows, rows)] = got[3 * rows :]
+            pbuf[st, lax.rem(k, 3), m, pl.ds(rows, rows)] = got[3 * rows :, lanes]
 
         op_copy(st, 0, k).start()
         op_copy(st, 1, k).start()

time: 105 us -> 105 us (level)
  no operation moved by 1% of the time
where the time goes in v4:
time: 105 us
  Pallas kernels  103 us (98%)
  local copies, waits for them, and re-layouts  2.02 us (2%)
    pallas_call x1, Pallas kernels, on_device(): pl.pallas_call(functools.partial(kernel, dims), out_shape=(pltpu.VMEM((ro...  103 us

profile of v4, /device:TPU:1, one launch (start us, length us, event | category | flops | bytes accessed | tf_op | source)
XLA Modules:
  0.0 105.3 jit_solution(971802910288702125)
XLA Ops:
  0.6 102.6 %shard_map.59 = (bf16[256,16,256]{2,1,0:T(8,128)(2,1)S(1)}, f32[256,256]{1,0:T(8,128)S(1)}) custom-call(bf16[256,16,2048]{2,1,0:T(8,128)(2,1)} %integrals.1, s32[16,32]{1,0:T(8,128)} %bitcast.1, bf16[2048,256]{1,0:T(8,128)(2,1)} %coeffs.1, bf16[256,4096]{1,0:T(8,128)(2,1)} %metric.1), custom_call_target="tpu_custom_call" | custom-call | flops 13421772800 | bytes 18874368 | tf_op jit(solution)/shard_map/pallas_call | solution.py:673
  103.3 1.3 %copy.8 = bf16[256,16,256]{2,1,0:T(8,128)(2,1)} copy(bf16[256,16,256]{2,1,0:T(8,128)(2,1)S(1)} %get-tuple-element.2) | data formatting | bytes 4194304
  104.6 0.7 copy.9

commit v5 on v2

--- a/solution.py
+++ b/solution.py
@@ -26,7 +26,7 @@
     ibuf, cbuf, cmask, stage_a, stage_b, mb, mbt, hbuf, opp_out, side_out, opp_in, side_in,
     rows_f32, out_bf16, pbuf, pair_acc, red0, mine, red1, red2, red3, red4,
     in_sem, c_sem, m_loc, m_send, m_recv, m2_send, m2_recv, m3_send, m3_recv,
-    ag_send, ag_recv, fw_send, fw_recv, op_send, op_recv, sd_send, sd_recv,
+    ag_send, ag_recv, fw_send, fw_recv, op_send, op_recv, sp_send, sp_recv, sd_send, sd_recv,
     r0_send, r0_recv, r1_send, r1_recv, r2_send, r2_recv, r3_send, r3_recv,
     r4_send, r4_recv, out_sem,
 ):
@@ -229,10 +229,22 @@
             device_id_type=MESH,
         )
 
+    def sp_copy(st, side, k):
+        part_rows = pl.ds((1 - side) * half, half)
+        return pltpu.make_async_remote_copy(
+            src_ref=side_out.at[side, mus(st, k), part_rows],
+            dst_ref=side_in.at[side, mus(st, k), part_rows],
+            send_sem=sp_send.at[st, side, k],
+            recv_sem=sp_recv.at[st, side, k],
+            device_id=(row, rs_to[st][side]),
+            device_id_type=MESH,
+        )
+
     def sd_copy(st, side, mu):
-        return pltpu.make_async_remote_copy(
-            src_ref=side_out.at[side, mu],
-            dst_ref=side_in.at[side, mu],
+        part_rows = pl.ds(side * half, half)
+        return pltpu.make_async_remote_copy(
+            src_ref=side_out.at[side, mu, part_rows],
+            dst_ref=side_in.at[side, mu, part_rows],
             send_sem=sd_send.at[side, mu],
             recv_sem=sd_recv.at[side, mu],
             device_id=(row, rs_to[st][side]),
@@ -270,8 +282,10 @@
                 pbuf[st, lax.rem(k, 3), m, pl.ds(side * half, half)] = (first, second)[side]
             pbuf[st, lax.rem(k, 3), m, pl.ds(rows, rows)] = got[3 * rows :]
 
-        op_copy(st, 0, k).start()
-        op_copy(st, 1, k).start()
+        for side in range(2):
+            op_copy(st, side, k).start()
+        for side in range(2):
+            sp_copy(st, side, k).start()
 
     def sides(k):
         for m in range(UNIT):
@@ -289,6 +303,10 @@
     pair_acc[...] = jnp.zeros_like(pair_acc)
 
     def finish(k):
+        for st in range(2):
+            for side in range(2):
+                sp_copy(st, side, k).wait_recv()
+
         @pl.loop(0, UNIT)
         def _(m):
             pairs = []
@@ -312,8 +330,9 @@
 
     quarter = rows // 4
 
-    def send_quarter(qt):
-        part_rows = pl.ds(pl.multiple_of(qt * quarter, quarter), quarter)
+    def send_rows(begin, count):
+        part_rows = pl.ds(pl.multiple_of(begin, QC), count)
+        hf = lax.div(begin, half)
         for k in range(AHEAD):
             for st in range(2):
                 for side in range(2):
@@ -322,8 +341,8 @@
                         dst_ref=hbuf.at[
                             mus(st, k), (at_x[0], (LEFT, RIGHT)[side])[st], part_rows
                         ],
-                        send_sem=ag_send.at[st, side, k, lax.div(qt, 2)],
-                        recv_sem=ag_recv.at[st, side, k, lax.div(qt, 2)],
+                        send_sem=ag_send.at[st, side, k, hf],
+                        recv_sem=ag_recv.at[st, side, k, hf],
                         device_id=(row, ag_to[st][side]),
                         device_id_type=MESH,
                     ).start()
@@ -346,9 +365,13 @@
         transform(ch, ab, stage_a)
         relayout(lax.max(ch - 1, 0), stage_b)
 
-        @pl.when(j >= 1)
-        def _():
-            send_quarter(j - 1)
+        @pl.when(j == 1)
+        def _():
+            send_rows(QC, quarter - QC)
+
+        @pl.when(j >= 2)
+        def _():
+            send_rows((j - 1) * quarter, quarter)
 
         @pl.when(j == 1)
         def _():
@@ -361,13 +384,17 @@
         transform(ch + 1, ab, stage_b)
         relayout(ch, stage_a)
 
+        @pl.when(j == 0)
+        def _():
+            send_rows(0, QC)
+
         @pl.when(ch + NBUF < nch)
         def _():
             in_copy(ch + NBUF).start()
             in_copy(ch + NBUF + 1).start()
 
     relayout(nch - 1, stage_b)
-    send_quarter(nch // 2 - 1)
+    send_rows((nch // 2 - 1) * quarter, quarter)
 
     def metric_sent():
         for s in range(1, NY):
@@ -388,6 +415,7 @@
     def sent_late(k):
         for st in range(2):
             for side in range(2):
+                sp_copy(st, side, k).wait_send()
                 for m in range(UNIT):
                     sd_copy(st, side, st * per_set + k * UNIT + m).wait_send()
 
@@ -425,10 +453,6 @@
                     m_shared(s, d).wait_recv()
                     m_pass(s, d).start()
 
-        @pl.when(k == nset + LAG - 1)
-        def _():
-            sides(k - LAG - 1)
-
         @pl.when((k >= LAG) & (k < nset + LAG))
         def _():
             @pl.when(k == LAG)
@@ -443,12 +467,9 @@
 
             product(1, k - LAG)
 
-        @pl.when((k >= LAG + 1) & (k < nset + LAG + 1) & (k != nset + LAG - 1))
+        @pl.when((k >= LAG + 1) & (k < nset + LAG + 1))
         def _():
             sides(k - LAG - 1)
-
-        @pl.when((k >= LAG + 1) & (k < nset + LAG + 1))
-        def _():
             sent_early(k - LAG - 1)
 
         @pl.when(k == LAG + 1)
@@ -668,6 +689,8 @@
         dma((2, 2, nmu // 2 // UNIT)),
         dma((2, 2, nmu // 2 // UNIT)),
         dma((2, 2, nmu // 2 // UNIT)),
+        dma((2, 2, nmu // 2 // UNIT)),
+        dma((2, 2, nmu // 2 // UNIT)),
         dma((2, nmu)),
         dma((2, nmu)),
         dma,

time: 107 us -> 106 us (level)
    pallas_call x1, Pallas kernels: 104 us -> 103 us  [on_device(): pl.pallas_call(functools.partial(kernel, dims), out_shape=(pltpu.VMEM((ro...]
where the time goes in v5:
time: 106 us
  Pallas kernels  103 us (97%)
  local copies, waits for them, and re-layouts  2.02 us (2%)
    pallas_call x1, Pallas kernels, on_device(): pl.pallas_call(functools.partial(kernel, dims), out_shape=(pltpu.VMEM((ro...  103 us

profile of v5, /device:TPU:1, one launch (start us, length us, event | category | flops | bytes accessed | tf_op | source)
XLA Modules:
  0.0 105.9 jit_solution(2171444537908284145)
XLA Ops:
  0.6 103.2 %shard_map.59 = (bf16[256,16,256]{2,1,0:T(8,128)(2,1)S(1)}, f32[256,256]{1,0:T(8,128)S(1)}) custom-call(bf16[256,16,2048]{2,1,0:T(8,128)(2,1)} %integrals.1, s32[16,32]{1,0:T(8,128)} %bitcast.1, bf16[2048,256]{1,0:T(8,128)(2,1)} %coeffs.1, bf16[256,4096]{1,0:T(8,128)(2,1)} %metric.1), custom_call_target="tpu_custom_call" | custom-call | flops 13421772800 | bytes 18874368 | tf_op jit(solution)/shard_map/pallas_call | solution.py:710
  103.8 1.3 %copy.8 = bf16[256,16,256]{2,1,0:T(8,128)(2,1)} copy(bf16[256,16,256]{2,1,0:T(8,128)(2,1)S(1)} %get-tuple-element.2) | data formatting | bytes 4194304
  105.2 0.7 copy.9

commit v6 on v1

--- a/solution.py
+++ b/solution.py
@@ -11,9 +11,12 @@
 NX = 4
 NY = 4
 QC = 32
-UNIT = 2
-AHEAD = 2
-LAG = 1
+UNIT = 1
+AHEAD = 4
+LAG = 2
+SIDES = LAG + 2
+FINISH = SIDES + 2
+RING = FINISH - LAG + 1
 NBUF = 4
 OPP, RIGHT, LEFT, OWN = range(4)
 MESH = pl.DeviceIdType.MESH
@@ -266,8 +269,8 @@
                 second = got[at + half : at + rows]
                 plain = pl.ds((1 - side) * half, half)
                 side_out[side, mu, plain] = (second, first)[side].astype(BF16)
-                pbuf[st, lax.rem(k, 3), m, pl.ds(side * half, half)] = (first, second)[side]
-            pbuf[st, lax.rem(k, 3), m, pl.ds(rows, rows)] = got[3 * rows :]
+                pbuf[st, lax.rem(k, RING), m, pl.ds(side * half, half)] = (first, second)[side]
+            pbuf[st, lax.rem(k, RING), m, pl.ds(rows, rows)] = got[3 * rows :]
 
         op_copy(st, 0, k).start()
         op_copy(st, 1, k).start()
@@ -281,7 +284,7 @@
                         op_copy(st, side, k).wait_recv()
                     at = pl.ds(side * half, half)
                     side_out[side, mu, at] = (
-                        pbuf[st, lax.rem(k, 3), m, at] + opp_in[mu, at].astype(F32)
+                        pbuf[st, lax.rem(k, RING), m, at] + opp_in[mu, at].astype(F32)
                     ).astype(BF16)
                     sd_copy(st, side, mu).start()
 
@@ -296,7 +299,7 @@
                     sd_copy(st, side, st * per_set + k * UNIT + m).wait_recv()
             for st in range(2):
                 mu = st * per_set + k * UNIT + m
-                own = pbuf[st, lax.rem(k, 3), m, pl.ds(rows, rows)]
+                own = pbuf[st, lax.rem(k, RING), m, pl.ds(rows, rows)]
                 total = own + side_in[0, mu].astype(F32) + side_in[1, mu].astype(F32)
                 done = total.astype(BF16)
                 back = done.astype(F32)
@@ -398,7 +401,7 @@
             def _(s):
                 mbt[to, :, pl.ds(pl.multiple_of(s * rows, 128), rows)] = mb[s, :, at].T
 
-    @pl.loop(0, nset + LAG + 2)
+    @pl.loop(0, nset + FINISH)
     def _(k):
         @pl.when(k + AHEAD < nset)
         def _():
@@ -410,7 +413,7 @@
             forward(0, k)
             forward(1, k)
 
-        @pl.when(k == 0)
+        @pl.when(k == LAG - 1)
         def _():
             for s in (2, 1, 3):
                 for d in (1, 3, 2):
@@ -431,22 +434,22 @@
 
             product(1, k - LAG)
 
-        @pl.when((k >= LAG + 1) & (k < nset + LAG + 1))
-        def _():
-            sides(k - LAG - 1)
-            sent_early(k - LAG - 1)
-
-        @pl.when(k == LAG + 1)
+        @pl.when((k >= SIDES) & (k < nset + SIDES))
+        def _():
+            sides(k - SIDES)
+            sent_early(k - SIDES)
+
+        @pl.when(k == SIDES)
         def _():
             metric_sent()
 
-        @pl.when(k >= LAG + 2)
-        def _():
-            finish(k - LAG - 2)
-
-        @pl.when((k >= LAG + 2) & (k < nset + LAG + 1))
-        def _():
-            sent_late(k - LAG - 2)
+        @pl.when(k >= FINISH)
+        def _():
+            finish(k - FINISH)
+
+        @pl.when((k >= FINISH) & (k < nset + FINISH - 1))
+        def _():
+            sent_late(k - FINISH)
 
     chunk = no // 2 // ncol
     core = lax.rem(row, 2)
@@ -630,7 +633,7 @@
         pltpu.VMEM((2, nmu, rows, no), BF16),
         pltpu.VMEM((lanes, rows * nmu, 128), F32),
         pltpu.VMEM((rows, nmu, no), BF16),
-        pltpu.VMEM((2, 3, UNIT, 2 * rows, no), F32),
+        pltpu.VMEM((2, RING, UNIT, 2 * rows, no), F32),
         pltpu.VMEM((no, no), F32),
         pltpu.VMEM((no // 2, no), F32),
         pltpu.VMEM((ncol, chunk, no), F32),

time: 105 us -> 107 us (1.019)
    pallas_call x1, Pallas kernels: 103 us -> 104 us  [on_device(): pl.pallas_call(functools.partial(kernel, dims), out_shape=(pltpu.VMEM((ro...]
where the time goes in v6:
time: 107 us; the launch traced here: 106 us
  Pallas kernels  104 us (97%)
  local copies, waits for them, and re-layouts  2.02 us (2%)
    pallas_call x1, Pallas kernels, on_device(): pl.pallas_call(functools.partial(kernel, dims), out_shape=(pltpu.VMEM((ro...  104 us

profile of v6, /device:TPU:1, one launch (start us, length us, event | category | flops | bytes accessed | tf_op | source)
XLA Modules:
  0.0 106.5 jit_solution(9625303340335270478)
XLA Ops:
  0.6 103.8 %shard_map.59 = (bf16[256,16,256]{2,1,0:T(8,128)(2,1)S(1)}, f32[256,256]{1,0:T(8,128)S(1)}) custom-call(bf16[256,16,2048]{2,1,0:T(8,128)(2,1)} %integrals.1, s32[16,32]{1,0:T(8,128)} %bitcast.1, bf16[2048,256]{1,0:T(8,128)(2,1)} %coeffs.1, bf16[256,4096]{1,0:T(8,128)(2,1)} %metric.1), custom_call_target="tpu_custom_call" | custom-call | flops 13421772800 | bytes 18874368 | tf_op jit(solution)/shard_map/pallas_call | solution.py:675
  104.5 1.3 %copy.8 = bf16[256,16,256]{2,1,0:T(8,128)(2,1)} copy(bf16[256,16,256]{2,1,0:T(8,128)(2,1)S(1)} %get-tuple-element.2) | data formatting | bytes 4194304
  105.8 0.7 copy.9

commit v7 on v2

--- a/solution.py
+++ b/solution.py
@@ -425,10 +425,6 @@
                     m_shared(s, d).wait_recv()
                     m_pass(s, d).start()
 
-        @pl.when(k == nset + LAG - 1)
-        def _():
-            sides(k - LAG - 1)
-
         @pl.when((k >= LAG) & (k < nset + LAG))
         def _():
             @pl.when(k == LAG)
@@ -443,12 +439,9 @@
 
             product(1, k - LAG)
 
-        @pl.when((k >= LAG + 1) & (k < nset + LAG + 1) & (k != nset + LAG - 1))
+        @pl.when((k >= LAG + 1) & (k < nset + LAG + 1))
         def _():
             sides(k - LAG - 1)
-
-        @pl.when((k >= LAG + 1) & (k < nset + LAG + 1))
-        def _():
             sent_early(k - LAG - 1)
 
         @pl.when(k == LAG + 1)
@@ -556,7 +549,7 @@
     r0_copy.wait_recv()
     mine[...] = (pair_acc[mine_at] + red0[...]).reshape(ncol, chunk, no)
 
-    @pl.loop(1, ncol, unroll=5)
+    @pl.loop(1, ncol, unroll=ncol - 1)
     def _(d):
         r1_copy(d).start()
 
@@ -568,7 +561,7 @@
     out_copy = pltpu.make_async_copy(out_bf16, fitted, out_sem)
     out_copy.start()
 
-    @pl.loop(1, ncol)
+    @pl.loop(1, ncol, unroll=ncol - 1)
     def _(d):
         r1_landed(lax.rem(col + d, ncol)).wait_recv()
 
@@ -586,11 +579,11 @@
         total = total + red2[z]
     red3[col] = total * F32(scale)
 
-    @pl.loop(1, ncol, unroll=5)
+    @pl.loop(1, ncol, unroll=ncol - 1)
     def _(d):
         r3_copy(d).start()
 
-    @pl.loop(1, ncol, unroll=5)
+    @pl.loop(1, ncol, unroll=ncol - 1)
     def _(d):
         r3_landed(lax.rem(col + d, ncol)).wait_recv()
 

time: 107 us -> 106 us (level)
    pallas_call x1, Pallas kernels: 104 us -> 103 us  [on_device(): pl.pallas_call(functools.partial(kernel, dims), out_shape=(pltpu.VMEM((ro...]
where the time goes in v7:
time: 106 us
  Pallas kernels  103 us (97%)
  local copies, waits for them, and re-layouts  2.02 us (2%)
    pallas_call x1, Pallas kernels, on_device(): pl.pallas_call(functools.partial(kernel, dims), out_shape=(pltpu.VMEM((ro...  103 us

profile of v7, /device:TPU:1, one launch (start us, length us, event | category | flops | bytes accessed | tf_op | source)
XLA Modules:
  0.0 105.5 jit_solution(10750349602388727667)
XLA Ops:
  0.6 102.9 %shard_map.59 = (bf16[256,16,256]{2,1,0:T(8,128)(2,1)S(1)}, f32[256,256]{1,0:T(8,128)S(1)}) custom-call(bf16[256,16,2048]{2,1,0:T(8,128)(2,1)} %integrals.1, s32[16,32]{1,0:T(8,128)} %bitcast.1, bf16[2048,256]{1,0:T(8,128)(2,1)} %coeffs.1, bf16[256,4096]{1,0:T(8,128)(2,1)} %metric.1), custom_call_target="tpu_custom_call" | custom-call | flops 13421772800 | bytes 18874368 | tf_op jit(solution)/shard_map/pallas_call | solution.py:680
  103.5 1.3 %copy.8 = bf16[256,16,256]{2,1,0:T(8,128)(2,1)} copy(bf16[256,16,256]{2,1,0:T(8,128)(2,1)S(1)} %get-tuple-element.2) | data formatting | bytes 4194304
  104.8 0.7 copy.9
